TPU v7x, 1024 devices: a whole 4x8x16 slice. The times are simulated.
1024 devices in a mesh: mode: 32 (over y_hi, x, core), space: 32 (over z, y_lo).
Axes of the slice: x: 4, y: 8 (y_hi: 4, y_lo: 2; y = y_hi * 2 + y_lo), z: 16, core: 2. Of those that a mesh axis runs over, the one named last changes fastest.
Arguments:
- left_modes: bfloat16 [2048, 24, 4096], P('mode', None, 'space'), may hold values from -6 to 6
- right_modes: bfloat16 [2048, 24, 4096], P('mode', None, 'space'), may hold values from -6 to 6
- momenta: int32 [8, 3], replicated, may hold values from -3 to 3
- spin_perm: int32 [8, 4], replicated, may hold values from 0 to 3, each once within a row
- spin_phase: int32 [8, 4], replicated, may hold values from 0 to 3
Outputs:
- fields: float32 [64, 2048, 64], P('space', 'mode')
Inputs may be any that keep to these rules, and one draw needn't show every extreme that they name: `spin_perm`: each row is a permutation of 0 to 3.
All inputs are finite; a program needn't handle non-finite values.
Results may differ from a plain program's by a relative error of at most 0.0028.
Values may be sent and summed in bfloat16 or wider, within the bound.
A program may use at most 32 MiB of HBM per device.

v0:
```python
import math

import jax
import jax.numpy as jnp
from jax import lax
from jax.sharding import PartitionSpec as P

STRUCTS = 8
CYCLE = 4
LAT = 96
BOX = 16


def from_behind(block, axis, distance):
    devices = range(lax.axis_size(axis))
    route = [((i - distance) % len(devices), i) for i in devices]
    return lax.ppermute(block, axis, route)


def turned_rows(mode_rows, momenta, spin_perm, spin_phase, coords, struct_id):
    mode_count = mode_rows.shape[0]
    site_count = mode_rows.shape[2]
    real_part = mode_rows[:, :12, :].astype(jnp.float32).reshape(mode_count, 4, 3, site_count)
    imag_part = mode_rows[:, 12:, :].astype(jnp.float32).reshape(mode_count, 4, 3, site_count)
    momentum_dot = jnp.sum(momenta[struct_id][:, None] * coords, axis=0)
    quarter = jnp.mod(LAT // 4 * spin_phase[struct_id][:, None] - momentum_dot[None, :], LAT)
    phase_angle = quarter.astype(jnp.float32) * (2.0 * math.pi / LAT)
    cosine = jnp.cos(phase_angle)[None, :, None, :]
    sine_val = jnp.sin(phase_angle)[None, :, None, :]
    turn_re = real_part * cosine + imag_part * sine_val
    turn_im = imag_part * cosine - real_part * sine_val
    chooser = (spin_perm[struct_id][:, None] == jnp.arange(4, dtype=jnp.int32)[None, :]).astype(
        jnp.float32
    )
    moved_re = chooser[0][None, :, None, None] * turn_re[:, 0:1]
    moved_im = chooser[0][None, :, None, None] * turn_im[:, 0:1]
    for spin_from in range(1, 4):
        moved_re = (
            moved_re
            + chooser[spin_from][None, :, None, None] * turn_re[:, spin_from : spin_from + 1]
        )
        moved_im = (
            moved_im
            + chooser[spin_from][None, :, None, None] * turn_im[:, spin_from : spin_from + 1]
        )
    re_rows = jnp.concatenate([moved_re, moved_im], axis=1).reshape(mode_count, 24, site_count)
    im_rows = jnp.concatenate([-moved_im, moved_re], axis=1).reshape(mode_count, 24, site_count)
    stacked = jnp.stack([re_rows, im_rows]).astype(jnp.bfloat16)
    return stacked.reshape(2 * mode_count, 24 * site_count)


def local(left_modes, right_modes, momenta, spin_perm, spin_phase):
    mode_count, comp_count, site_count = left_modes.shape
    space_count = lax.axis_size("space")
    out_rows = STRUCTS * CYCLE * 2 // space_count
    site_index = lax.axis_index("space") * site_count + lax.iota(jnp.int32, site_count)
    coords = jnp.stack([site_index % BOX, site_index // BOX % BOX, site_index // (BOX * BOX)])
    blocks = [right_modes]
    current = right_modes
    for shift_step in range(1, CYCLE):
        current = from_behind(current, "mode", 1)
        blocks.append(current)
    rights = jnp.stack(blocks).reshape(CYCLE * mode_count, comp_count * site_count)
    all_rows = jnp.concatenate(
        [
            turned_rows(left_modes, momenta, spin_perm, spin_phase, coords, struct_id)
            for struct_id in range(STRUCTS)
        ],
        axis=0,
    )
    product = lax.dot_general(
        all_rows, rights, (((1,), (1,)), ((), ())), preferred_element_type=jnp.float32
    )
    partial_value = product.reshape(STRUCTS, 2, mode_count, CYCLE, mode_count).transpose(
        0, 3, 1, 2, 4
    )
    partial_value = partial_value.reshape(STRUCTS * CYCLE * 2, mode_count, mode_count)
    summed = lax.psum(partial_value, "space")
    owned = lax.dynamic_slice_in_dim(summed, lax.axis_index("space") * out_rows, out_rows, 0)
    factor = 1.0 / math.sqrt(24 * site_count * space_count)
    return owned * factor


def solution(mesh):
    placed = (P("mode", None, "space"), P("mode", None, "space"), P(), P(), P())
    return jax.shard_map(
        local, mesh=mesh, in_specs=placed, out_specs=P("space", "mode", None), check_vma=False
    )
```

profile of v0, /device:TPU:6, one launch (start us, length us, event | category | flops | bytes accessed | tf_op | source)
XLA Modules:
  0.0 362.1 jit_solution(16499082896718902919)
XLA Ops:
  6.5 2.0 collective-permute-start
  8.6 1.2 stack.62
  9.8 1.3 slice_reduce_fusion
  11.1 1.3 multiply_reduce_fusion.1
  12.4 1.1 fusion.98
  13.6 0.1 multiply_reduce_fusion
  13.7 0.1 fusion.79
  13.8 0.1 fusion.81
  14.0 0.1 fusion.83
  14.1 0.1 fusion.85
  14.2 0.1 fusion.87
  14.3 0.1 fusion.89
  14.5 0.1 fusion.91
  14.6 0.1 fusion.93
  14.7 1.0 fusion.21
  15.8 0.3 slice_reduce_fusion.1
  16.1 0.1 fusion.76
  16.1 0.3 fusion.22
  16.5 0.1 pad_maximum_fusion.7
  16.6 0.5 copy.29
  17.2 0.3 fusion.23
  17.6 0.1 pad_maximum_fusion.6
  17.7 0.5 copy.28
  18.3 0.1 fusion.74
  18.4 0.3 fusion.24
  18.7 0.1 pad_maximum_fusion.18
  18.7 0.1 pad_maximum_fusion.5
  18.8 0.5 copy.27
  19.4 0.3 fusion.25
  19.8 0.1 pad_maximum_fusion.4
  19.9 0.5 copy.26
  20.5 0.1 fusion.72
  20.6 0.3 fusion.26
  20.9 0.1 pad_maximum_fusion.3
  21.0 0.5 copy.25
  21.6 0.3 fusion.27
  22.0 0.1 pad_maximum_fusion.2
  22.1 0.5 copy.24
  22.7 0.1 fusion.70
  22.8 0.3 fusion.28
  23.1 0.1 pad_maximum_fusion.1
  23.2 0.5 copy.23
  23.8 0.3 fusion.29
  24.2 0.1 pad_maximum_fusion
  24.3 0.5 copy.22
  24.8 1.0 bitcast_dynamic-update-slice_fusion.7
  25.8 1.0 bitcast_dynamic-update-slice_fusion.6
  26.8 1.0 bitcast_dynamic-update-slice_fusion.5
  27.8 1.0 bitcast_dynamic-update-slice_fusion.4
  28.8 1.0 bitcast_dynamic-update-slice_fusion.3
  29.8 1.0 bitcast_dynamic-update-slice_fusion.2
  30.8 4.5 %collective-permute-start.1 = (bf16[64,24,128]{2,1,0:T(8,128)(2,1)S(1)}, bf16[64,24,128]{2,1,0:T(8,128)(2,1)S(1)}, u32[]{:S(2)}, u32[]{:S(2)}) collective-permute-start(bf16[64,24,128]{2,1,0:T(8,128)(2,1)S(1)} %collective-permute-done), channel_id=1, source_target_pairs={{992,0},{0,32},{32,64},{64,96},{96,128},{128,160},{160,192},{192,2... | collective-permute-start | bytes 1179656 | tf_op jit(solution)/shard_map/ppermute | solution.py:17
  35.3 1.0 bitcast_dynamic-update-slice_fusion.1
  36.3 3.6 collective-permute-done.1
  39.9 6.2 %collective-permute-start.2 = (bf16[64,24,128]{2,1,0:T(8,128)(2,1)S(1)}, bf16[64,24,128]{2,1,0:T(8,128)(2,1)S(1)}, u32[]{:S(2)}, u32[]{:S(2)}) collective-permute-start(bf16[64,24,128]{2,1,0:T(8,128)(2,1)S(1)} %collective-permute-done.1), channel_id=1, source_target_pairs={{992,0},{0,32},{32,64},{64,96},{96,128},{128,160},{160,192},{192,2... | collective-permute-start | bytes 1179656 | tf_op jit(solution)/shard_map/ppermute | solution.py:17
  46.2 1.1 bitcast_dynamic-update-slice_fusion
  47.2 0.2 stack.63
  47.4 0.2 stack.64
  47.6 1.4 collective-permute-done.2
  49.0 0.2 stack.65
  49.2 5.5 %convolution_bitcast_fusion = f32[8,4,2,64,64]{4,3,1,2,0:T(8,128)S(1)} fusion(bf16[8,2,64,3072,1]{3,2,4,1,0:T(8,128)(2,1)} %bitcast.118, bf16[1,64,3072]{2,1,0:T(8,128)(2,1)S(1)} %stack.65, bf16[1,64,3072]{2,1,0:T(8,128)(2,1)S(1)} %stack.64, bf16[1,64,3072]{2,1,0:T(8,128)(2,1)S(1)} %stack.63, bf16[1,64,3072]{2,1,0:T(8,128)(2,1)S(1)} %stack.62), kind=kOutput, calls=%fused_computation.32 | convolution fusion | flops 1616904192 | bytes 8912896 | tf_op jit(solution)/shard_map/dot_general | solution.py:71
  54.7 1.4 copy.30
  56.2 297.6 %all-reduce.2.cloned.1.call-done = f32[64,64,64]{2,1,0:T(8,128)} async-done(((f32[64,64,64]{2,1,0:T(8,128)}), f32[64,64,64]{2,1,0:T(8,128)}) %all-reduce.2.cloned.1.call-update) | async-done | bytes 1048592 | tf_op jit(solution)/shard_map/psum | solution.py:78
  353.7 1.5 dynamic-slice_multiply_fusion
  (40 shorter events, 1.1 us)
Async XLA Ops:
  6.5 9.2 %copy-start = (s32[8,4]{0,1:T(4,128)S(1)}, s32[8,4]{0,1:T(4,128)}, u32[]{:S(2)}) copy-start(s32[8,4]{0,1:T(4,128)} %param.8) | copy-start | bytes 388
  6.5 347.2 %all-reduce.2.cloned.1.call-start = ((), (), s32[]{:S(2)}) async-start(), calls=%async_computation | async-start | bytes 4194304 | tf_op jit(solution)/shard_map/psum | solution.py:78
  6.5 24.3 %collective-permute-start = (bf16[64,24,128]{2,1,0:T(8,128)(2,1)}, bf16[64,24,128]{2,1,0:T(8,128)(2,1)S(1)}, u32[]{:S(2)}, u32[]{:S(2)}) collective-permute-start(bf16[64,24,128]{2,1,0:T(8,128)(2,1)} %param.6), channel_id=1, source_target_pairs={{992,0},{0,32},{32,64},{64,96},{96,128},{128,160},{160,192},{192,2... | collective-permute-start | bytes 1179656 | tf_op jit(solution)/shard_map/ppermute | solution.py:17
  30.8 9.1 %collective-permute-start.1 = (bf16[64,24,128]{2,1,0:T(8,128)(2,1)S(1)}, bf16[64,24,128]{2,1,0:T(8,128)(2,1)S(1)}, u32[]{:S(2)}, u32[]{:S(2)}) collective-permute-start(bf16[64,24,128]{2,1,0:T(8,128)(2,1)S(1)} %collective-permute-done), channel_id=1, source_target_pairs={{992,0},{0,32},{32,64},{64,96},{96,128},{128,160},{160,192},{192,2... | collective-permute-start | bytes 1179656 | tf_op jit(solution)/shard_map/ppermute | solution.py:17
  39.9 9.1 %collective-permute-start.2 = (bf16[64,24,128]{2,1,0:T(8,128)(2,1)S(1)}, bf16[64,24,128]{2,1,0:T(8,128)(2,1)S(1)}, u32[]{:S(2)}, u32[]{:S(2)}) collective-permute-start(bf16[64,24,128]{2,1,0:T(8,128)(2,1)S(1)} %collective-permute-done.1), channel_id=1, source_target_pairs={{992,0},{0,32},{32,64},{64,96},{96,128},{128,160},{160,192},{192,2... | collective-permute-start | bytes 1179656 | tf_op jit(solution)/shard_map/ppermute | solution.py:17
Sparse Core Ops, SparseCore 0:
  56.3 297.3 all-reduce.1
where the time goes:
time: 363 us; the launch traced here: 362 us
  waiting for transfers between devices  303 us (83%)
  local copies, waits for them, and re-layouts  18.6 us (5%)
  between operations  13.9 us (4%)
  starting transfers between devices  12.8 us (4%)
  other arithmetic  8.65 us (2%)
  matrix products  5.55 us (2%)
    psum x1, waiting for transfers between devices, local(): summed = lax.psum(partial_value, 'space')  298 us
    ppermute x3, starting transfers between devices, from_behind(): return lax.ppermute(block, axis, route)  12.8 us
  transfers between devices with their start and end apart: 4, of which 3 were waited for; matrix products, arithmetic and copies ran while one was open for 7% of the time, Pallas kernels for 0%

commit v1 on v0

v1 whole, which is shorter than its diff:
```python
import math

import jax
import jax.numpy as jnp
from jax import lax
from jax.experimental import pallas as pl
from jax.experimental.pallas import tpu as pltpu
from jax.sharding import PartitionSpec as P

STRUCTS = 8
LAT = 96
BOX = 16
MODES = 64
COMP = 24
PAIRS = 12
SITES = 128
PARTS = 4
PER = PAIRS // PARTS
NZ = 16
FLOAT = jnp.float32
HALF = jnp.bfloat16
MESH = pl.DeviceIdType.MESH


def kernel(
    momenta,
    perm,
    phase,
    left_hbm,
    right_hbm,
    out_ref,
    left_raw,
    right_raw,
    wide,
    angle,
    cosine,
    sine,
    left_own,
    left_far,
    right_own,
    right_far,
    rows,
    sums,
    send_one,
    take_one,
    send_two,
    take_two,
    load_sem,
    right_send,
    right_take,
    left_send,
    left_take,
    one_send,
    one_take,
    two_send,
    two_take,
):
    n_mode = lax.axis_size("mode")
    mode = lax.axis_index("mode")
    space = lax.axis_index("space")
    z = space // 2
    y = space % 2
    odd = z % 2

    def modes_on(step):
        return lax.rem(mode + step + n_mode, n_mode)

    def along(step):
        return lax.rem(z + step + NZ, NZ)

    load_left = pltpu.make_async_copy(left_hbm, left_raw, load_sem.at[0])
    load_right = pltpu.make_async_copy(right_hbm, right_raw, load_sem.at[1])
    load_right.start()
    load_left.start()

    barrier = pltpu.get_barrier_semaphore()

    def greet(to_mode, to_space):
        pl.semaphore_signal(barrier, inc=1, device_id=(to_mode, to_space), device_id_type=MESH)

    greet(modes_on(-2), space)
    greet(modes_on(1), space)
    for step in (-2, -1, 1, 2):
        greet(mode, along(step) * 2 + y)
    for turn in range(4):
        far = along(4 * turn)

        @pl.when(jnp.logical_or(y == 1, turn != 0))
        def _():
            greet(modes_on(0 - y), far * 2)

        greet(modes_on(0 - y), far * 2 + 1)

    lane = lax.broadcasted_iota(jnp.int32, (1, SITES), 1)
    first = lane % BOX
    second = (space * (SITES // BOX) + lane // BOX) % BOX
    third = space * SITES // (BOX * BOX)
    sources = []
    for struct in range(STRUCTS):
        dot = momenta[0, struct] * first + momenta[1, struct] * second + momenta[2, struct] * third
        own = []
        for spin in range(4):
            origin = jnp.int32(0)
            for other in range(1, 4):
                origin = jnp.where(perm[other, struct] == spin, other, origin)
            turn = phase[0, struct]
            for other in range(1, 4):
                turn = jnp.where(origin == other, phase[other, struct], turn)
            value = LAT // 4 * turn - dot + 2 * LAT
            quarter = value
            for times in range(1, 5):
                quarter = quarter - jnp.where(value >= times * LAT, LAT, 0)
            angle[pl.ds(struct * 4 + spin, 1), :] = quarter.astype(FLOAT) * (2.0 * math.pi / LAT)
            own.append(origin)
        sources.append(own)
    cosine[...] = jnp.cos(angle[...])
    sine[...] = jnp.sin(angle[...])

    def spread(raw):
        def step(part, carry):
            piece = raw[pl.ds(part * 8, 8)].astype(FLOAT).reshape(8 * COMP, SITES)
            wide[pl.ds(pl.multiple_of(part * 8 * COMP, 8 * COMP), 8 * COMP), :] = piece
            return carry

        lax.fori_loop(0, MODES // 8, step, 0)

    def component(index):
        return wide[pl.ds(index, MODES, stride=COMP), :]

    load_right.wait()
    spread(right_raw)
    for pair in range(PAIRS):
        real, imag = component(pair), component(PAIRS + pair)
        right_own[pair, :MODES, :SITES] = real.astype(HALF)
        right_own[pair, :MODES, SITES:] = imag.astype(HALF)
        right_own[pair, MODES:, :SITES] = imag.astype(HALF)
        right_own[pair, MODES:, SITES:] = (-real).astype(HALF)
    load_left.wait()
    spread(left_raw)
    for pair in range(PAIRS):
        left_own[pair, :, :SITES] = component(pair).astype(HALF)
        left_own[pair, :, SITES:] = component(PAIRS + pair).astype(HALF)

    @pl.when(y == 0)
    def _():
        pl.semaphore_wait(barrier, 13)

    @pl.when(y == 1)
    def _():
        pl.semaphore_wait(barrier, 14)

    left_copy = pltpu.make_async_remote_copy(
        left_own, left_far, left_send, left_take, (modes_on(-1), space), MESH
    )
    right_copies = [
        pltpu.make_async_remote_copy(
            right_own.at[pl.ds(part * PER, PER), pl.ds(0, MODES)],
            right_far.at[pl.ds(part * PER, PER), pl.ds(0, MODES)],
            right_send.at[part],
            right_take.at[part],
            (modes_on(2), space),
            MESH,
        )
        for part in range(PARTS)
    ]
    left_copy.start()
    for copy in right_copies:
        copy.start()

    def turn_rows(li):
        for struct in range(STRUCTS):
            for spin in range(4):
                origin = sources[struct][spin]
                turn_re = cosine[pl.ds(struct * 4 + spin, 1), :]
                turn_im = sine[pl.ds(struct * 4 + spin, 1), :]
                for colour in range(3):
                    block = (left_own, left_far)[li][origin * 3 + colour]
                    real = block[:, :SITES].astype(FLOAT)
                    imag = block[:, SITES:].astype(FLOAT)
                    place = rows.at[spin * 3 + colour, li * STRUCTS + struct]
                    place[:, :SITES] = (real * turn_re + imag * turn_im).astype(HALF)
                    place[:, SITES:] = (imag * turn_re - real * turn_im).astype(HALF)

    def multiply(li, rj, start, stop):
        def step(pair, carry):
            block = rows[pair, pl.ds(li * STRUCTS, STRUCTS)].reshape(STRUCTS * MODES, 2 * SITES)
            product = lax.dot_general(
                block, (right_own, right_far)[rj][pair], (((1,), (1,)), ((), ())), preferred_element_type=FLOAT
            )
            sums[rj, li] = sums[rj, li] + product.reshape(STRUCTS, MODES, 2 * MODES)
            return carry

        lax.fori_loop(start, stop, step, 0)

    def pack(li, rj):
        for struct in range(STRUCTS):
            send_one[rj, struct % 2, struct // 2, li] = sums[rj, li, struct].astype(HALF)

    def one_copies(rj):
        halfs = [lax.rem(z + NZ + step, 4) // 2 for step in (-1, 1, 2)]
        near = [
            pltpu.make_async_remote_copy(
                send_one.at[rj, halfs[side]],
                take_one.at[1 - side],
                one_send.at[rj, side],
                one_take.at[1 - side],
                (mode, along((-1, 1)[side]) * 2 + y),
                MESH,
            )
            for side in range(2)
        ]
        beyond = [
            pltpu.make_async_remote_copy(
                send_one.at[rj, halfs[2], pl.ds(2 * side, 2)],
                take_one.at[2, pl.ds(2 * side, 2)],
                one_send.at[rj, side],
                one_take.at[2 + side],
                (mode, along((2, -2)[side]) * 2 + y),
                MESH,
            )
            for side in range(2)
        ]
        return near, beyond

    def send_sums(rj):
        near, beyond = one_copies(rj)

        @pl.when(odd != rj)
        def _():
            for copy in near:
                copy.start()

        @pl.when(odd == rj)
        def _():
            for copy in beyond:
                copy.start()

    own_q = z // 4
    own_h = z % 4 // 2

    def two_copy(q, li):
        return pltpu.make_async_remote_copy(
            send_two.at[q, li],
            take_two.at[own_q, y],
            two_send.at[q, li],
            two_take.at[own_q, y],
            (modes_on(li), (q * 4 + z % 4) * 2 + li),
            MESH,
        )

    def pass_sums(rj):
        near, beyond = one_copies(rj)

        @pl.when(odd == rj)
        def _():
            for copy in near + beyond:
                copy.wait_recv()
            for q in range(4):
                for li in range(2):
                    total = sums[rj, li, q * 2 + own_h]
                    for slot in range(3):
                        total = total + take_one[slot, q, li].astype(FLOAT)
                    send_two[q, li] = total.astype(HALF)
                    if li == 0:
                        mine = jnp.logical_and(q == own_q, y == 0)

                        @pl.when(mine)
                        def _():
                            take_two[own_q, 0] = total.astype(HALF)

                        @pl.when(jnp.logical_not(mine))
                        def _():
                            two_copy(q, li).start()
                    else:
                        two_copy(q, li).start()

    sums[...] = jnp.zeros_like(sums)
    turn_rows(0)
    multiply(0, 0, 0, PAIRS)
    pack(0, 0)
    left_copy.wait_recv()
    turn_rows(1)
    multiply(1, 0, 0, PAIRS)
    pack(1, 0)
    send_sums(0)
    pass_sums(0)
    for part in range(PARTS):
        right_copies[part].wait_recv()
        for pair in range(part * PER, part * PER + PER):
            block = right_far[pair, :MODES, :]
            right_far[pair, MODES:, :SITES] = block[:, SITES:]
            right_far[pair, MODES:, SITES:] = (-block[:, :SITES].astype(FLOAT)).astype(HALF)
        for li in range(2):
            multiply(li, 1, part * PER, part * PER + PER)
    for li in range(2):
        pack(li, 1)
    send_sums(1)
    pass_sums(1)

    def two_wait(q, from_y):
        pltpu.make_async_remote_copy(
            send_two.at[0, 0],
            take_two.at[q, from_y],
            two_send.at[0, 0],
            two_take.at[q, from_y],
            (mode, space),
            MESH,
        ).wait_recv()

    total = jnp.zeros((MODES, 2 * MODES), FLOAT)
    for q in range(4):
        for from_y in range(2):
            if from_y == 0:

                @pl.when(jnp.logical_not(jnp.logical_and(q == own_q, y == 0)))
                def _():
                    two_wait(q, from_y)
            else:
                two_wait(q, from_y)
            total = total + take_two[q, from_y].astype(FLOAT)
    total = total * (1.0 / math.sqrt(COMP * SITES * NZ * 2))
    out_ref[0] = total[:, :MODES]
    out_ref[1] = total[:, MODES:]

    left_copy.wait_send()
    for copy in right_copies:
        copy.wait_send()
    for rj in range(2):
        near, beyond = one_copies(rj)

        @pl.when(odd != rj)
        def _():
            for copy in near:
                copy.wait_send()

        @pl.when(odd == rj)
        def _():
            for copy in beyond:
                copy.wait_send()

    for q in range(4):
        for li in range(2):

            @pl.when(jnp.logical_not(jnp.logical_and(jnp.logical_and(q == own_q, y == 0), li == 0)))
            def _():
                two_copy(q, li).wait_send()


def solution(mesh):
    def local(left_modes, right_modes, momenta, spin_perm, spin_phase):
        small = pl.BlockSpec(memory_space=pltpu.SMEM)
        large = pl.BlockSpec(memory_space=pl.ANY)
        dma = pltpu.SemaphoreType.DMA
        return pl.pallas_call(
            kernel,
            out_shape=jax.ShapeDtypeStruct((2, MODES, MODES), FLOAT),
            in_specs=[small, small, small, large, large],
            out_specs=pl.BlockSpec(memory_space=pltpu.VMEM),
            scratch_shapes=[
                pltpu.VMEM((MODES, COMP, SITES), HALF),
                pltpu.VMEM((MODES, COMP, SITES), HALF),
                pltpu.VMEM((MODES * COMP, SITES), FLOAT),
                pltpu.VMEM((STRUCTS * 4, SITES), FLOAT),
                pltpu.VMEM((STRUCTS * 4, SITES), FLOAT),
                pltpu.VMEM((STRUCTS * 4, SITES), FLOAT),
                pltpu.VMEM((PAIRS, MODES, 2 * SITES), HALF),
                pltpu.VMEM((PAIRS, MODES, 2 * SITES), HALF),
                pltpu.VMEM((PAIRS, 2 * MODES, 2 * SITES), HALF),
                pltpu.VMEM((PAIRS, 2 * MODES, 2 * SITES), HALF),
                pltpu.VMEM((PAIRS, 2 * STRUCTS, MODES, 2 * SITES), HALF),
                pltpu.VMEM((2, 2, STRUCTS, MODES, 2 * MODES), FLOAT),
                pltpu.VMEM((2, 2, 4, 2, MODES, 2 * MODES), HALF),
                pltpu.VMEM((3, 4, 2, MODES, 2 * MODES), HALF),
                pltpu.VMEM((4, 2, MODES, 2 * MODES), HALF),
                pltpu.VMEM((4, 2, MODES, 2 * MODES), HALF),
                dma((2,)),
                dma((PARTS,)),
                dma((PARTS,)),
                dma,
                dma,
                dma((2, 2)),
                dma((4,)),
                dma((4, 2)),
                dma((4, 2)),
            ],
            compiler_params=pltpu.CompilerParams(
                collective_id=0, has_side_effects=True, vmem_limit_bytes=40 * 2**20
            ),
            cost_estimate=pl.CostEstimate(
                flops=2 * 1024 * 256 * 3072, bytes_accessed=2**20, transcendentals=8192
            ),
        )(momenta.T, spin_perm.T, spin_phase.T, left_modes, right_modes)

    placed = (P("mode", None, "space"), P("mode", None, "space"), P(), P(), P())
    return jax.shard_map(
        local, mesh=mesh, in_specs=placed, out_specs=P("space", "mode", None), check_vma=False
    )
```

time: 363 us -> 67.1 us (0.18)
  the two profiles are of different devices: /device:TPU:6 before, /device:TPU:72 now
where the time goes in v1:
time: 67.1 us; the launch traced here: 66.9 us
  Pallas kernels  62.9 us (94%)
  local copies, waits for them, and re-layouts  4 us (6%)
    pallas_call x1, Pallas kernels, local(): pl.pallas_call(kernel, out_shape=jax.ShapeDtypeStruct((2, MODES, MODES),...  62.9 us
    unnamed x11, local copies, waits for them, and re-layouts  4 us

profile of v1, /device:TPU:72, one launch (start us, length us, event | category | flops | bytes accessed | tf_op | source)
XLA Modules:
  0.0 66.9 jit_solution(15874715812706186547)
XLA Ops:
  0.0 0.0 copy-start.3
  0.0 0.0 copy-start.2
  0.0 0.7 %copy-done.3 = s32[8,4]{0,1:T(4,128)S(1)} copy-done((s32[8,4]{0,1:T(4,128)S(1)}, s32[8,4]{0,1:T(4,128)}, u32[]{:S(2)}) %copy-start.3) | copy-done | bytes 152
  0.7 0.0 copy-done.2
  0.7 0.0 copy-start
  0.7 1.0 %copy-done = bf16[64,24,128]{2,1,0:T(8,128)(2,1)S(1)} copy-done((bf16[64,24,128]{2,1,0:T(8,128)(2,1)S(1)}, bf16[64,24,128]{2,1,0:T(8,128)(2,1)}, u32[]{:S(2)}) %copy-start) | copy-done | bytes 393240
  1.7 0.0 copy-start.1
  1.7 1.0 %copy-done.1 = bf16[64,24,128]{2,1,0:T(8,128)(2,1)S(1)} copy-done((bf16[64,24,128]{2,1,0:T(8,128)(2,1)S(1)}, bf16[64,24,128]{2,1,0:T(8,128)(2,1)}, u32[]{:S(2)}) %copy-start.1) | copy-done | bytes 393240
  2.7 0.0 copy-start.4
  2.7 0.7 %copy-done.4 = s32[8,4]{0,1:T(4,128)S(1)} copy-done((s32[8,4]{0,1:T(4,128)S(1)}, s32[8,4]{0,1:T(4,128)}, u32[]{:S(2)}) %copy-start.4) | copy-done | bytes 152
  3.4 62.9 %shard_map.55 = f32[2,64,64]{2,1,0:T(8,128)S(1)} custom-call(s32[3,8]{1,0:T(4,128)S(1)} %bitcast.3, s32[4,8]{1,0:T(4,128)S(1)} %bitcast.4, s32[4,8]{1,0:T(4,128)S(1)} %bitcast.5, bf16[64,24,128]{2,1,0:T(8,128)(2,1)S(1)} %copy-done, bf16[64,24,128]{2,1,0:T(8,128)(2,1)S(1)} %copy-done.1), custom_call_target="tpu_custom_call" | custom-call | flops 1610612736 | bytes 1048576 | tf_op jit(solution)/shard_map/pallas_call | solution.py:354
  66.3 0.6 copy.7
Async XLA Ops:
  0.0 0.7 %copy-start.3 = (s32[8,4]{0,1:T(4,128)S(1)}, s32[8,4]{0,1:T(4,128)}, u32[]{:S(2)}) copy-start(s32[8,4]{0,1:T(4,128)} %param.8) | copy-start | bytes 388
  0.0 0.7 %copy-start.2 = (s32[8,3]{0,1:T(4,128)S(1)}, s32[8,3]{0,1:T(4,128)}, u32[]{:S(2)}) copy-start(s32[8,3]{0,1:T(4,128)} %param.7) | copy-start | bytes 292
  0.7 1.0 %copy-start = (bf16[64,24,128]{2,1,0:T(8,128)(2,1)S(1)}, bf16[64,24,128]{2,1,0:T(8,128)(2,1)}, u32[]{:S(2)}) copy-start(bf16[64,24,128]{2,1,0:T(8,128)(2,1)} %left_hbm.1) | copy-start | bytes 1179652
  1.7 1.0 %copy-start.1 = (bf16[64,24,128]{2,1,0:T(8,128)(2,1)S(1)}, bf16[64,24,128]{2,1,0:T(8,128)(2,1)}, u32[]{:S(2)}) copy-start(bf16[64,24,128]{2,1,0:T(8,128)(2,1)} %right_hbm.1) | copy-start | bytes 1179652
  2.7 0.7 %copy-start.4 = (s32[8,4]{0,1:T(4,128)S(1)}, s32[8,4]{0,1:T(4,128)}, u32[]{:S(2)}) copy-start(s32[8,4]{0,1:T(4,128)} %param.9) | copy-start | bytes 388

commit v2 on v1

v2 whole, which is shorter than its diff:
```python
import math

import jax
import jax.numpy as jnp
from jax import lax
from jax.experimental import pallas as pl
from jax.experimental.pallas import tpu as pltpu
from jax.sharding import PartitionSpec as P

STRUCTS = 8
LAT = 96
BOX = 16
MODES = 64
COMP = 24
PAIRS = 12
SITES = 128
PARTS = 6
PER = PAIRS // PARTS
RELAYED = (3, 4, 5)
NZ = 16
ROW = 8
SLOTS = 6
FLOAT = jnp.float32
HALF = jnp.bfloat16
MESH = pl.DeviceIdType.MESH


def kernel(
    momenta_hbm,
    perm_hbm,
    phase_hbm,
    left_hbm,
    right_hbm,
    out_ref,
    momenta,
    perm,
    phase,
    left_raw,
    right_raw,
    wide,
    angle,
    cosine,
    sine,
    left_own,
    left_far,
    right_own,
    right_far,
    relay,
    rows,
    sums,
    send_one,
    take_one,
    send_two,
    take_two,
    load_sem,
    right_send,
    right_take,
    relay_take,
    relay_send,
    left_send,
    left_take,
    one_send,
    one_take,
    two_send,
    two_take,
):
    n_mode = lax.axis_size("mode")
    mode = lax.axis_index("mode")
    space = lax.axis_index("space")
    z = space // 2
    y = space % 2
    odd = z % 2
    in_row = lax.rem(mode, ROW)
    first_chip = in_row < 2
    last_chip = in_row >= ROW - 2

    def modes_on(step):
        return lax.rem(mode + step + n_mode, n_mode)

    def along(step):
        return lax.rem(z + step + NZ, NZ)

    loads = [
        pltpu.make_async_copy(source, target, load_sem.at[index])
        for index, (source, target) in enumerate(
            (
                (right_hbm, right_raw),
                (left_hbm, left_raw),
                (momenta_hbm, momenta),
                (perm_hbm, perm),
                (phase_hbm, phase),
            )
        )
    ]
    for load in loads:
        load.start()

    barrier = pltpu.get_barrier_semaphore()

    def greet(to_mode, to_space):
        pl.semaphore_signal(barrier, inc=1, device_id=(to_mode, to_space), device_id_type=MESH)

    greet(modes_on(-2), space)
    greet(modes_on(1), space)

    @pl.when(first_chip)
    def _():
        greet(mode + ROW - 2, space)
        greet(modes_on(-ROW), space)

    for step in (-2, -1, 1, 2, 3):
        greet(mode, along(step) * 2 + y)
    for step in (0, 5, -5):
        if step == 0:

            @pl.when(y == 1)
            def _():
                greet(modes_on(0 - y), z * 2)
        else:
            greet(modes_on(0 - y), along(step) * 2)
        greet(modes_on(0 - y), along(step) * 2 + 1)

    def spread(raw):
        def step(part, carry):
            piece = raw[pl.ds(part * 8, 8)].astype(FLOAT).reshape(8 * COMP, SITES)
            wide[pl.ds(pl.multiple_of(part * 8 * COMP, 8 * COMP), 8 * COMP), :] = piece
            return carry

        lax.fori_loop(0, MODES // 8, step, 0)

    def component(index):
        return wide[pl.ds(index, MODES, stride=COMP), :]

    loads[0].wait()
    spread(right_raw)
    for pair in range(PAIRS):
        real, imag = component(pair), component(PAIRS + pair)
        right_own[pair, :MODES, :SITES] = real.astype(HALF)
        right_own[pair, :MODES, SITES:] = imag.astype(HALF)
        right_own[pair, MODES:, :SITES] = imag.astype(HALF)
        right_own[pair, MODES:, SITES:] = (-real).astype(HALF)
    loads[1].wait()
    spread(left_raw)
    for pair in range(PAIRS):
        left_own[pair, :, :SITES] = component(pair).astype(HALF)
        left_own[pair, :, SITES:] = component(PAIRS + pair).astype(HALF)

    edge = jnp.logical_or(first_chip, last_chip)
    pl.semaphore_wait(barrier, 12 + y + edge.astype(jnp.int32))

    def part_of(ref, part):
        return ref.at[pl.ds(part * PER, PER), pl.ds(0, MODES)]

    def right_copy(part):
        return pltpu.make_async_remote_copy(
            part_of(right_own, part),
            part_of(right_far, part),
            right_send.at[part],
            right_take.at[part],
            (modes_on(2), space),
            MESH,
        )

    def aside_copy(turn):
        return pltpu.make_async_remote_copy(
            part_of(right_own, RELAYED[turn]),
            relay.at[turn],
            right_send.at[RELAYED[turn]],
            relay_take.at[turn],
            (modes_on(2 - ROW), space),
            MESH,
        )

    def relay_copy(turn):
        return pltpu.make_async_remote_copy(
            relay.at[turn],
            part_of(right_far, RELAYED[turn]),
            relay_send.at[turn],
            right_take.at[RELAYED[turn]],
            (modes_on(ROW), space),
            MESH,
        )

    left_copy = pltpu.make_async_remote_copy(
        left_own, left_far, left_send, left_take, (modes_on(-1), space), MESH
    )

    @pl.when(last_chip)
    def _():
        for turn in range(len(RELAYED)):
            aside_copy(turn).start()

    for part in range(PARTS):
        if part not in RELAYED:
            right_copy(part).start()
    left_copy.start()

    @pl.when(jnp.logical_not(last_chip))
    def _():
        for part in RELAYED:
            right_copy(part).start()

    for load in loads[2:]:
        load.wait()

    lane = lax.broadcasted_iota(jnp.int32, (1, SITES), 1)
    first = lane % BOX
    second = (space * (SITES // BOX) + lane // BOX) % BOX
    third = space * SITES // (BOX * BOX)
    sources = []
    for struct in range(STRUCTS):
        dot = momenta[0, struct] * first + momenta[1, struct] * second + momenta[2, struct] * third
        own = []
        for spin in range(4):
            origin = jnp.int32(0)
            for other in range(1, 4):
                origin = jnp.where(perm[other, struct] == spin, other, origin)
            turn = phase[0, struct]
            for other in range(1, 4):
                turn = jnp.where(origin == other, phase[other, struct], turn)
            value = LAT // 4 * turn - dot + 2 * LAT
            quarter = value
            for times in range(1, 5):
                quarter = quarter - jnp.where(value >= times * LAT, LAT, 0)
            angle[pl.ds(struct * 4 + spin, 1), :] = quarter.astype(FLOAT) * (2.0 * math.pi / LAT)
            own.append(origin)
        sources.append(own)
    cosine[...] = jnp.cos(angle[...])
    sine[...] = jnp.sin(angle[...])

    def turn_rows(li):
        for struct in range(STRUCTS):
            for spin in range(4):
                origin = sources[struct][spin]
                turn_re = cosine[pl.ds(struct * 4 + spin, 1), :]
                turn_im = sine[pl.ds(struct * 4 + spin, 1), :]
                for colour in range(3):
                    block = (left_own, left_far)[li][origin * 3 + colour]
                    real = block[:, :SITES].astype(FLOAT)
                    imag = block[:, SITES:].astype(FLOAT)
                    place = rows.at[spin * 3 + colour, li, struct]
                    place[:, :SITES] = (real * turn_re + imag * turn_im).astype(HALF)
                    place[:, SITES:] = (imag * turn_re - real * turn_im).astype(HALF)

    def product(blocks, right, pairs):
        total = None
        for pair in pairs:
            left = jnp.concatenate(
                [rows[pair, li, a:b].reshape((b - a) * MODES, 2 * SITES) for li, a, b in blocks], axis=0
            )
            term = lax.dot_general(
                left, right[pair], (((1,), (1,)), ((), ())), preferred_element_type=FLOAT
            )
            total = term if total is None else total + term
        return total.reshape(-1, MODES, 2 * MODES)

    def near_sums(li):
        total = product([(li, 0, STRUCTS)], right_own, range(PAIRS))
        sums[0, li] = total
        for struct in range(STRUCTS):
            send_one[0, struct, li] = total[struct].astype(HALF)

    def far_arrive(parts):
        for part in parts:
            right_copy(part).wait_recv()
            for pair in range(part * PER, part * PER + PER):
                block = right_far[pair, :MODES, :]
                right_far[pair, MODES:, :SITES] = block[:, SITES:]
                right_far[pair, MODES:, SITES:] = (-block[:, :SITES].astype(FLOAT)).astype(HALF)

    def far_sums(li, pairs, fresh):
        total = product([(li, 0, STRUCTS)], right_far, pairs)
        sums[1, li] = total if fresh else sums[1, li] + total

    def one_place(rj, struct):
        to = 2 * struct + rj
        gap = lax.rem(z - to + NZ, NZ)
        plus = jnp.logical_and(gap >= 3, gap <= 8)
        minus = jnp.logical_and(gap >= 9, gap <= 13)
        role = jnp.where(plus, 1, jnp.where(minus, 2, 0))
        adder = lax.rem(to + jnp.where(plus, 5, jnp.where(minus, NZ - 5, 0)), NZ)
        slot = lax.rem(z - adder + NZ + 2, NZ)
        return adder, role, slot

    def one_copy(rj, struct):
        adder, role, slot = one_place(rj, struct)
        return adder != z, pltpu.make_async_remote_copy(
            send_one.at[rj, struct],
            take_one.at[role, slot],
            one_send.at[rj, struct],
            one_take.at[role, slot],
            (mode, adder * 2 + y),
            MESH,
        )

    def send_sums(rj, struct):
        away, copy = one_copy(rj, struct)

        @pl.when(away)
        def _():
            copy.start()

    def owner_z(role):
        return along((0, -5, 5)[role])

    def two_copy(role, li):
        return pltpu.make_async_remote_copy(
            send_two.at[role, li],
            take_two.at[role, y],
            two_send.at[role, li],
            two_take.at[role, y],
            (modes_on(li), owner_z(role) * 2 + li),
            MESH,
        )

    def add_and_pass(role):
        slots = (0, 1, 3, 4, 5) if role == 1 else (0, 1, 3, 4)
        for slot in slots:
            pltpu.make_async_remote_copy(
                send_one.at[0, 0],
                take_one.at[role, slot],
                one_send.at[0, 0],
                one_take.at[role, slot],
                (mode, space),
                MESH,
            ).wait_recv()
        to = owner_z(role)
        for li in range(2):
            total = sums[to % 2, li, to // 2]
            for slot in slots:
                total = total + take_one[role, slot, li].astype(FLOAT)
            send_two[role, li] = total.astype(HALF)
            if role == 0 and li == 0:

                @pl.when(y == 0)
                def _():
                    take_two[0, 0] = total.astype(HALF)

                @pl.when(y == 1)
                def _():
                    two_copy(role, li).start()
            else:
                two_copy(role, li).start()

    def pass_sums(rj):
        @pl.when(odd == rj)
        def _():
            add_and_pass(0)

        @pl.when(odd != rj)
        def _():
            add_and_pass(1)
            add_and_pass(2)

    def hand_on(turn):
        @pl.when(first_chip)
        def _():
            aside_copy(turn).wait_recv()
            relay_copy(turn).start()

    turn_rows(0)
    hand_on(0)
    near_sums(0)
    hand_on(1)
    left_copy.wait_recv()
    turn_rows(1)
    hand_on(2)
    near_sums(1)
    for struct in range(STRUCTS):
        send_sums(0, struct)
    far_arrive((0, 1, 2))
    for li in range(2):
        far_sums(li, range(0, 3 * PER), True)
    pass_sums(0)
    far_arrive((3, 4))
    for li in range(2):
        far_sums(li, range(3 * PER, 5 * PER), False)
    far_arrive((5,))
    for q in range(STRUCTS // 2):
        last = product([(0, 2 * q, 2 * q + 2), (1, 2 * q, 2 * q + 2)], right_far, range(5 * PER, PAIRS))
        for struct in (2 * q, 2 * q + 1):
            for li in range(2):
                total = sums[1, li, struct] + last[2 * li + struct % 2]
                sums[1, li, struct] = total
                send_one[1, struct, li] = total.astype(HALF)
            send_sums(1, struct)
    pass_sums(1)

    total = jnp.zeros((MODES, 2 * MODES), FLOAT)
    for role in range(3):
        for from_y in range(2):
            arrived = pltpu.make_async_remote_copy(
                send_two.at[0, 0],
                take_two.at[role, from_y],
                two_send.at[0, 0],
                two_take.at[role, from_y],
                (mode, space),
                MESH,
            )
            if role == 0 and from_y == 0:

                @pl.when(y == 1)
                def _():
                    arrived.wait_recv()
            else:
                arrived.wait_recv()
            total = total + take_two[role, from_y].astype(FLOAT)
    total = total * (1.0 / math.sqrt(COMP * SITES * NZ * 2))
    out_ref[0] = total[:, :MODES]
    out_ref[1] = total[:, MODES:]

    left_copy.wait_send()
    for part in range(PARTS):
        right_copy(part).wait_send()

    @pl.when(first_chip)
    def _():
        for turn in range(len(RELAYED)):
            relay_copy(turn).wait_send()

    for rj in range(2):
        for struct in range(STRUCTS):
            away, copy = one_copy(rj, struct)

            @pl.when(away)
            def _():
                copy.wait_send()

    for role in range(3):
        for li in range(2):
            if role == 0 and li == 0:

                @pl.when(y == 1)
                def _():
                    two_copy(role, li).wait_send()
            else:
                two_copy(role, li).wait_send()


def solution(mesh):
    def local(left_modes, right_modes, momenta, spin_perm, spin_phase):
        large = pl.BlockSpec(memory_space=pl.ANY)
        dma = pltpu.SemaphoreType.DMA
        return pl.pallas_call(
            kernel,
            out_shape=jax.ShapeDtypeStruct((2, MODES, MODES), FLOAT),
            in_specs=[large] * 5,
            out_specs=pl.BlockSpec(memory_space=pltpu.VMEM),
            scratch_shapes=[
                pltpu.SMEM((3, STRUCTS), jnp.int32),
                pltpu.SMEM((4, STRUCTS), jnp.int32),
                pltpu.SMEM((4, STRUCTS), jnp.int32),
                pltpu.VMEM((MODES, COMP, SITES), HALF),
                pltpu.VMEM((MODES, COMP, SITES), HALF),
                pltpu.VMEM((MODES * COMP, SITES), FLOAT),
                pltpu.VMEM((STRUCTS * 4, SITES), FLOAT),
                pltpu.VMEM((STRUCTS * 4, SITES), FLOAT),
                pltpu.VMEM((STRUCTS * 4, SITES), FLOAT),
                pltpu.VMEM((PAIRS, MODES, 2 * SITES), HALF),
                pltpu.VMEM((PAIRS, MODES, 2 * SITES), HALF),
                pltpu.VMEM((PAIRS, 2 * MODES, 2 * SITES), HALF),
                pltpu.VMEM((PAIRS, 2 * MODES, 2 * SITES), HALF),
                pltpu.VMEM((len(RELAYED), PER, MODES, 2 * SITES), HALF),
                pltpu.VMEM((PAIRS, 2, STRUCTS, MODES, 2 * SITES), HALF),
                pltpu.VMEM((2, 2, STRUCTS, MODES, 2 * MODES), FLOAT),
                pltpu.VMEM((2, STRUCTS, 2, MODES, 2 * MODES), HALF),
                pltpu.VMEM((3, SLOTS, 2, MODES, 2 * MODES), HALF),
                pltpu.VMEM((3, 2, MODES, 2 * MODES), HALF),
                pltpu.VMEM((3, 2, MODES, 2 * MODES), HALF),
                dma((5,)),
                dma((PARTS,)),
                dma((PARTS,)),
                dma((len(RELAYED),)),
                dma((len(RELAYED),)),
                dma,
                dma,
                dma((2, STRUCTS)),
                dma((3, SLOTS)),
                dma((3, 2)),
                dma((3, 2)),
            ],
            compiler_params=pltpu.CompilerParams(
                collective_id=0, has_side_effects=True, vmem_limit_bytes=60 * 2**20
            ),
            cost_estimate=pl.CostEstimate(
                flops=2 * 1024 * 256 * 3072, bytes_accessed=2**20, transcendentals=8192
            ),
        )(momenta.T, spin_perm.T, spin_phase.T, left_modes, right_modes)

    placed = (P("mode", None, "space"), P("mode", None, "space"), P(), P(), P())
    return jax.shard_map(
        local, mesh=mesh, in_specs=placed, out_specs=P("space", "mode", None), check_vma=False
    )
```

time: 67.1 us -> 56.5 us (0.84)
  Pallas kernels: 62.9 us -> 54.9 us
  local copies, waits for them, and re-layouts: 4 us -> 1.47 us
    pallas_call x1, Pallas kernels: 62.9 us -> 54.9 us  [local(): pl.pallas_call(kernel, out_shape=jax.ShapeDtypeStruct((2, MODES, MODES),...]
    unnamed x11 -> x1, local copies, waits for them, and re-layouts: 4 us -> 1.47 us
where the time goes in v2:
time: 56.5 us; the launch traced here: 56.3 us
  Pallas kernels  54.9 us (97%)
  local copies, waits for them, and re-layouts  1.47 us (3%)
    pallas_call x1, Pallas kernels, local(): pl.pallas_call(kernel, out_shape=jax.ShapeDtypeStruct((2, MODES, MODES),...  54.9 us
    unnamed x1, local copies, waits for them, and re-layouts  1.47 us

profile of v2, /device:TPU:72, one launch (start us, length us, event | category | flops | bytes accessed | tf_op | source)
XLA Modules:
  0.0 56.3 jit_solution(12523045211952350636)
XLA Ops:
  0.0 54.9 %shard_map.55 = f32[2,64,64]{2,1,0:T(8,128)} custom-call(s32[3,8]{1,0:T(4,128)} %bitcast.3, s32[4,8]{1,0:T(4,128)} %bitcast.4, s32[4,8]{1,0:T(4,128)} %bitcast.5, bf16[64,24,128]{2,1,0:T(8,128)(2,1)} %left_hbm.1, bf16[64,24,128]{2,1,0:T(8,128)(2,1)} %right_hbm.1), custom_call_target="tpu_custom_call" | custom-call | flops 1610612736 | bytes 1048576 | tf_op jit(solution)/shard_map/pallas_call | solution.py:444
  54.9 1.5 %copy.7 = f32[2,64,64]{2,1,0:T(8,128)} copy(f32[2,64,64]{2,1,0:T(8,128)} %shard_map.55) | data formatting | bytes 65536

commit v3 on v2

--- a/solution.py
+++ b/solution.py
@@ -14,12 +14,13 @@
 COMP = 24
 PAIRS = 12
 SITES = 128
-PARTS = 6
+PARTS = 12
 PER = PAIRS // PARTS
-RELAYED = (3, 4, 5)
+RELAYED = (8, 9, 10, 11)
+LEFT_CUTS = ((0, 8), (8, 2), (10, 2))
 NZ = 16
 ROW = 8
-SLOTS = 6
+SLOTS = 7
 FLOAT = jnp.float32
 HALF = jnp.bfloat16
 MESH = pl.DeviceIdType.MESH
@@ -46,6 +47,7 @@
     right_own,
     right_far,
     relay,
+    left_relay,
     rows,
     sums,
     send_one,
@@ -59,6 +61,8 @@
     relay_send,
     left_send,
     left_take,
+    aside_take,
+    aside_send,
     one_send,
     one_take,
     two_send,
@@ -92,25 +96,12 @@
             )
         )
     ]
-    for load in loads:
-        load.start()
-
     barrier = pltpu.get_barrier_semaphore()
 
     def greet(to_mode, to_space):
         pl.semaphore_signal(barrier, inc=1, device_id=(to_mode, to_space), device_id_type=MESH)
 
-    greet(modes_on(-2), space)
-    greet(modes_on(1), space)
-
-    @pl.when(first_chip)
-    def _():
-        greet(mode + ROW - 2, space)
-        greet(modes_on(-ROW), space)
-
-    for step in (-2, -1, 1, 2, 3):
-        greet(mode, along(step) * 2 + y)
-    for step in (0, 5, -5):
+    for step in (5, -5, 0):
         if step == 0:
 
             @pl.when(y == 1)
@@ -119,6 +110,25 @@
         else:
             greet(modes_on(0 - y), along(step) * 2)
         greet(modes_on(0 - y), along(step) * 2 + 1)
+
+    for load in loads:
+        load.start()
+
+    for step in (3, -3, -2, 2, -1, 1):
+        greet(mode, along(step) * 2 + y)
+
+    greet(modes_on(-2), space)
+    greet(modes_on(1), space)
+
+    @pl.when(first_chip)
+    def _():
+        greet(mode + ROW - 2, space)
+        greet(modes_on(-ROW), space)
+
+    @pl.when(in_row == ROW - 1)
+    def _():
+        greet(mode - ROW + 1, space)
+        greet(modes_on(ROW), space)
 
     def spread(raw):
         def step(part, carry):
@@ -146,7 +156,8 @@
         left_own[pair, :, SITES:] = component(PAIRS + pair).astype(HALF)
 
     edge = jnp.logical_or(first_chip, last_chip)
-    pl.semaphore_wait(barrier, 12 + y + edge.astype(jnp.int32))
+    ends = jnp.logical_or(in_row == 0, in_row == ROW - 1)
+    pl.semaphore_wait(barrier, 13 + y + edge.astype(jnp.int32) + ends.astype(jnp.int32))
 
     def part_of(ref, part):
         return ref.at[pl.ds(part * PER, PER), pl.ds(0, MODES)]
@@ -181,25 +192,69 @@
             MESH,
         )
 
-    left_copy = pltpu.make_async_remote_copy(
-        left_own, left_far, left_send, left_take, (modes_on(-1), space), MESH
-    )
-
-    @pl.when(last_chip)
-    def _():
-        for turn in range(len(RELAYED)):
+    def left_part(ref, cut):
+        start, size = LEFT_CUTS[cut]
+        return ref.at[pl.ds(start, size)]
+
+    def left_copy(cut):
+        return pltpu.make_async_remote_copy(
+            left_part(left_own, cut),
+            left_part(left_far, cut),
+            left_send.at[cut],
+            left_take.at[cut],
+            (modes_on(-1), space),
+            MESH,
+        )
+
+    def left_aside(cut):
+        return pltpu.make_async_remote_copy(
+            left_part(left_own, cut),
+            left_relay.at[cut - 1],
+            left_send.at[cut],
+            aside_take.at[cut - 1],
+            (modes_on(ROW - 1), space),
+            MESH,
+        )
+
+    def left_on(cut):
+        return pltpu.make_async_remote_copy(
+            left_relay.at[cut - 1],
+            left_part(left_far, cut),
+            aside_send.at[cut - 1],
+            left_take.at[cut],
+            (modes_on(-ROW), space),
+            MESH,
+        )
+
+    def start_aside(turn):
+        @pl.when(last_chip)
+        def _():
             aside_copy(turn).start()
+
+    start_aside(0)
+
+    @pl.when(in_row == 0)
+    def _():
+        left_aside(1).start()
+        left_aside(2).start()
+
+    left_copy(0).start()
+
+    @pl.when(in_row != 0)
+    def _():
+        left_copy(1).start()
+        left_copy(2).start()
 
     for part in range(PARTS):
         if part not in RELAYED:
             right_copy(part).start()
-    left_copy.start()
 
     @pl.when(jnp.logical_not(last_chip))
     def _():
         for part in RELAYED:
             right_copy(part).start()
 
+    start_aside(1)
     for load in loads[2:]:
         load.wait()
 
@@ -225,11 +280,13 @@
             angle[pl.ds(struct * 4 + spin, 1), :] = quarter.astype(FLOAT) * (2.0 * math.pi / LAT)
             own.append(origin)
         sources.append(own)
+        if struct % 4 == 3:
+            start_aside(2 + struct // 4)
     cosine[...] = jnp.cos(angle[...])
     sine[...] = jnp.sin(angle[...])
 
-    def turn_rows(li):
-        for struct in range(STRUCTS):
+    def turn_rows(li, structs):
+        for struct in structs:
             for spin in range(4):
                 origin = sources[struct][spin]
                 turn_re = cosine[pl.ds(struct * 4 + spin, 1), :]
@@ -275,11 +332,12 @@
     def one_place(rj, struct):
         to = 2 * struct + rj
         gap = lax.rem(z - to + NZ, NZ)
-        plus = jnp.logical_and(gap >= 3, gap <= 8)
-        minus = jnp.logical_and(gap >= 9, gap <= 13)
+        middle = 8 if to < NZ // 2 else 7
+        plus = jnp.logical_and(gap >= 3, gap <= middle)
+        minus = jnp.logical_and(gap > middle, gap <= 13)
         role = jnp.where(plus, 1, jnp.where(minus, 2, 0))
         adder = lax.rem(to + jnp.where(plus, 5, jnp.where(minus, NZ - 5, 0)), NZ)
-        slot = lax.rem(z - adder + NZ + 2, NZ)
+        slot = lax.rem(z - adder + NZ + 3, NZ)
         return adder, role, slot
 
     def one_copy(rj, struct):
@@ -314,7 +372,22 @@
         )
 
     def add_and_pass(role):
-        slots = (0, 1, 3, 4, 5) if role == 1 else (0, 1, 3, 4)
+        slots = (1, 2, 4, 5)
+        if role == 0:
+            add_slots(role, slots)
+            return
+        low = owner_z(role) < NZ // 2
+        more = low if role == 1 else jnp.logical_not(low)
+
+        @pl.when(more)
+        def _():
+            add_slots(role, slots + ((6,) if role == 1 else (0,)))
+
+        @pl.when(jnp.logical_not(more))
+        def _():
+            add_slots(role, slots)
+
+    def add_slots(role, slots):
         for slot in slots:
             pltpu.make_async_remote_copy(
                 send_one.at[0, 0],
@@ -349,8 +422,17 @@
 
         @pl.when(odd != rj)
         def _():
-            add_and_pass(1)
+            back = jnp.logical_and(z >= 5, z < 11)
+
+            @pl.when(back)
+            def _():
+                add_and_pass(1)
+
             add_and_pass(2)
+
+            @pl.when(jnp.logical_not(back))
+            def _():
+                add_and_pass(1)
 
     def hand_on(turn):
         @pl.when(first_chip)
@@ -358,26 +440,41 @@
             aside_copy(turn).wait_recv()
             relay_copy(turn).start()
 
-    turn_rows(0)
+    def left_hand_on(cut):
+        @pl.when(in_row == ROW - 1)
+        def _():
+            left_aside(cut).wait_recv()
+            left_on(cut).start()
+
+    turn_rows(0, range(0, 4))
+    if len(RELAYED) > 4:
+        start_aside(4)
+    turn_rows(0, range(4, STRUCTS))
+    if len(RELAYED) > 5:
+        start_aside(5)
     hand_on(0)
+    hand_on(1)
+    left_hand_on(1)
     near_sums(0)
-    hand_on(1)
-    left_copy.wait_recv()
-    turn_rows(1)
-    hand_on(2)
+    left_hand_on(2)
+    for turn in range(2, len(RELAYED)):
+        hand_on(turn)
+    for cut in range(len(LEFT_CUTS)):
+        left_copy(cut).wait_recv()
+    turn_rows(1, range(STRUCTS))
     near_sums(1)
     for struct in range(STRUCTS):
         send_sums(0, struct)
-    far_arrive((0, 1, 2))
+    far_arrive(range(0, 6))
     for li in range(2):
-        far_sums(li, range(0, 3 * PER), True)
+        far_sums(li, range(0, 6), True)
     pass_sums(0)
-    far_arrive((3, 4))
+    far_arrive(range(6, 10))
     for li in range(2):
-        far_sums(li, range(3 * PER, 5 * PER), False)
-    far_arrive((5,))
+        far_sums(li, range(6, 10), False)
+    far_arrive(range(10, PARTS))
     for q in range(STRUCTS // 2):
-        last = product([(0, 2 * q, 2 * q + 2), (1, 2 * q, 2 * q + 2)], right_far, range(5 * PER, PAIRS))
+        last = product([(0, 2 * q, 2 * q + 2), (1, 2 * q, 2 * q + 2)], right_far, range(10, PAIRS))
         for struct in (2 * q, 2 * q + 1):
             for li in range(2):
                 total = sums[1, li, struct] + last[2 * li + struct % 2]
@@ -409,7 +506,8 @@
     out_ref[0] = total[:, :MODES]
     out_ref[1] = total[:, MODES:]
 
-    left_copy.wait_send()
+    for cut in range(len(LEFT_CUTS)):
+        left_copy(cut).wait_send()
     for part in range(PARTS):
         right_copy(part).wait_send()
 
@@ -417,6 +515,11 @@
     def _():
         for turn in range(len(RELAYED)):
             relay_copy(turn).wait_send()
+
+    @pl.when(in_row == ROW - 1)
+    def _():
+        for cut in (1, 2):
+            left_on(cut).wait_send()
 
     for rj in range(2):
         for struct in range(STRUCTS):
@@ -461,6 +564,7 @@
                 pltpu.VMEM((PAIRS, 2 * MODES, 2 * SITES), HALF),
                 pltpu.VMEM((PAIRS, 2 * MODES, 2 * SITES), HALF),
                 pltpu.VMEM((len(RELAYED), PER, MODES, 2 * SITES), HALF),
+                pltpu.VMEM((2, 2, MODES, 2 * SITES), HALF),
                 pltpu.VMEM((PAIRS, 2, STRUCTS, MODES, 2 * SITES), HALF),
                 pltpu.VMEM((2, 2, STRUCTS, MODES, 2 * MODES), FLOAT),
                 pltpu.VMEM((2, STRUCTS, 2, MODES, 2 * MODES), HALF),
@@ -472,8 +576,10 @@
                 dma((PARTS,)),
                 dma((len(RELAYED),)),
                 dma((len(RELAYED),)),
-                dma,
-                dma,
+                dma((len(LEFT_CUTS),)),
+                dma((len(LEFT_CUTS),)),
+                dma((2,)),
+                dma((2,)),
                 dma((2, STRUCTS)),
                 dma((3, SLOTS)),
                 dma((3, 2)),

time: 56.5 us -> 53.4 us (0.945)
  the two profiles are of different devices: /device:TPU:72 before, /device:TPU:89 now
where the time goes in v3:
time: 53.4 us; the launch traced here: 53.2 us
  Pallas kernels  51.7 us (97%)
  local copies, waits for them, and re-layouts  1.47 us (3%)
    pallas_call x1, Pallas kernels, local(): pl.pallas_call(kernel, out_shape=jax.ShapeDtypeStruct((2, MODES, MODES),...  51.7 us
    unnamed x1, local copies, waits for them, and re-layouts  1.47 us

profile of v3, /device:TPU:89, one launch (start us, length us, event | category | flops | bytes accessed | tf_op | source)
XLA Modules:
  0.0 53.2 jit_solution(6761189999594127671)
XLA Ops:
  0.0 51.7 %shard_map.55 = f32[2,64,64]{2,1,0:T(8,128)} custom-call(s32[3,8]{1,0:T(4,128)} %bitcast.3, s32[4,8]{1,0:T(4,128)} %bitcast.4, s32[4,8]{1,0:T(4,128)} %bitcast.5, bf16[64,24,128]{2,1,0:T(8,128)(2,1)} %left_hbm.1, bf16[64,24,128]{2,1,0:T(8,128)(2,1)} %right_hbm.1), custom_call_target="tpu_custom_call" | custom-call | flops 1610612736 | bytes 1048576 | tf_op jit(solution)/shard_map/pallas_call | solution.py:547
  51.7 1.5 %copy.7 = f32[2,64,64]{2,1,0:T(8,128)} copy(f32[2,64,64]{2,1,0:T(8,128)} %shard_map.55) | data formatting | bytes 65536

commit v4 on v3

--- a/solution.py
+++ b/solution.py
@@ -468,7 +468,6 @@
     far_arrive(range(0, 6))
     for li in range(2):
         far_sums(li, range(0, 6), True)
-    pass_sums(0)
     far_arrive(range(6, 10))
     for li in range(2):
         far_sums(li, range(6, 10), False)
@@ -481,6 +480,7 @@
                 sums[1, li, struct] = total
                 send_one[1, struct, li] = total.astype(HALF)
             send_sums(1, struct)
+    pass_sums(0)
     pass_sums(1)
 
     total = jnp.zeros((MODES, 2 * MODES), FLOAT)

time: 53.4 us -> 51.9 us (0.972)
  the two profiles are of different devices: /device:TPU:89 before, /device:TPU:64 now
where the time goes in v4:
time: 51.9 us; the launch traced here: 51.7 us
  Pallas kernels  50.2 us (97%)
  local copies, waits for them, and re-layouts  1.47 us (3%)
    pallas_call x1, Pallas kernels, local(): pl.pallas_call(kernel, out_shape=jax.ShapeDtypeStruct((2, MODES, MODES),...  50.2 us
    unnamed x1, local copies, waits for them, and re-layouts  1.47 us

profile of v4, /device:TPU:64, one launch (start us, length us, event | category | flops | bytes accessed | tf_op | source)
XLA Modules:
  0.0 51.7 jit_solution(1869736258826797323)
XLA Ops:
  0.0 50.2 %shard_map.55 = f32[2,64,64]{2,1,0:T(8,128)} custom-call(s32[3,8]{1,0:T(4,128)} %bitcast.3, s32[4,8]{1,0:T(4,128)} %bitcast.4, s32[4,8]{1,0:T(4,128)} %bitcast.5, bf16[64,24,128]{2,1,0:T(8,128)(2,1)} %left_hbm.1, bf16[64,24,128]{2,1,0:T(8,128)(2,1)} %right_hbm.1), custom_call_target="tpu_custom_call" | custom-call | flops 1610612736 | bytes 1048576 | tf_op jit(solution)/shard_map/pallas_call | solution.py:547
  50.2 1.5 %copy.7 = f32[2,64,64]{2,1,0:T(8,128)} copy(f32[2,64,64]{2,1,0:T(8,128)} %shard_map.55) | data formatting | bytes 65536

commit v5 on v4

--- a/solution.py
+++ b/solution.py
@@ -586,12 +586,17 @@
                 dma((3, 2)),
             ],
             compiler_params=pltpu.CompilerParams(
-                collective_id=0, has_side_effects=True, vmem_limit_bytes=60 * 2**20
+                collective_id=0, has_side_effects=True, vmem_limit_bytes=40 * 2**20
             ),
             cost_estimate=pl.CostEstimate(
                 flops=2 * 1024 * 256 * 3072, bytes_accessed=2**20, transcendentals=8192
             ),
-        )(momenta.T, spin_perm.T, spin_phase.T, left_modes, right_modes)
+        )(
+            *(
+                pltpu.with_memory_space_constraint(array, pltpu.HBM)
+                for array in (momenta.T, spin_perm.T, spin_phase.T, left_modes, right_modes)
+            )
+        )
 
     placed = (P("mode", None, "space"), P("mode", None, "space"), P(), P(), P())
     return jax.shard_map(

time: 51.9 us -> 50.4 us (0.971)
  local copies, waits for them, and re-layouts: 1.47 us -> 0.63 us
  Pallas kernels: 50.2 us -> 49.6 us
    unnamed x1, local copies, waits for them, and re-layouts: 1.47 us -> 0.63 us
    pallas_call x1, Pallas kernels: 50.2 us -> 49.6 us  [local(): pl.pallas_call(kernel, out_shape=jax.ShapeDtypeStruct((2, MODES, MODES),...]
where the time goes in v5:
time: 50.4 us; the launch traced here: 50.2 us
  Pallas kernels  49.6 us (98%)
  local copies, waits for them, and re-layouts  0.63 us (1%)
    pallas_call x1, Pallas kernels, local(): pl.pallas_call(kernel, out_shape=jax.ShapeDtypeStruct((2, MODES, MODES),...  49.6 us

profile of v5, /device:TPU:64, one launch (start us, length us, event | category | flops | bytes accessed | tf_op | source)
XLA Modules:
  0.0 50.2 jit_solution(4010097146954140568)
XLA Ops:
  0.0 49.6 %shard_map.55 = f32[2,64,64]{2,1,0:T(8,128)S(1)} custom-call(s32[3,8]{1,0:T(4,128)} %bitcast.3, s32[4,8]{1,0:T(4,128)} %bitcast.4, s32[4,8]{1,0:T(4,128)} %bitcast.5, bf16[64,24,128]{2,1,0:T(8,128)(2,1)} %left_hbm.1, bf16[64,24,128]{2,1,0:T(8,128)(2,1)} %right_hbm.1), custom_call_target="tpu_custom_call" | custom-call | flops 1610612736 | bytes 1048576 | tf_op jit(solution)/shard_map/pallas_call | solution.py:547
  49.6 0.6 %copy.7 = f32[2,64,64]{2,1,0:T(8,128)} copy(f32[2,64,64]{2,1,0:T(8,128)S(1)} %shard_map.55) | data formatting | bytes 65536

commit v6 on v5

--- a/solution.py
+++ b/solution.py
@@ -455,10 +455,10 @@
     hand_on(0)
     hand_on(1)
     left_hand_on(1)
-    near_sums(0)
     left_hand_on(2)
     for turn in range(2, len(RELAYED)):
         hand_on(turn)
+    near_sums(0)
     for cut in range(len(LEFT_CUTS)):
         left_copy(cut).wait_recv()
     turn_rows(1, range(STRUCTS))

time: 50.4 us -> 51.9 us (1.030)
  the two profiles are of different devices: /device:TPU:64 before, /device:TPU:89 now
where the time goes in v6:
time: 51.9 us; the launch traced here: 51.8 us
  Pallas kernels  51.1 us (98%)
  local copies, waits for them, and re-layouts  0.63 us (1%)
    pallas_call x1, Pallas kernels, local(): pl.pallas_call(kernel, out_shape=jax.ShapeDtypeStruct((2, MODES, MODES),...  51.1 us

profile of v6, /device:TPU:89, one launch (start us, length us, event | category | flops | bytes accessed | tf_op | source)
XLA Modules:
  0.0 51.8 jit_solution(7732034193520451010)
XLA Ops:
  0.0 51.1 %shard_map.55 = f32[2,64,64]{2,1,0:T(8,128)S(1)} custom-call(s32[3,8]{1,0:T(4,128)} %bitcast.3, s32[4,8]{1,0:T(4,128)} %bitcast.4, s32[4,8]{1,0:T(4,128)} %bitcast.5, bf16[64,24,128]{2,1,0:T(8,128)(2,1)} %left_hbm.1, bf16[64,24,128]{2,1,0:T(8,128)(2,1)} %right_hbm.1), custom_call_target="tpu_custom_call" | custom-call | flops 1610612736 | bytes 1048576 | tf_op jit(solution)/shard_map/pallas_call | solution.py:547
  51.1 0.6 %copy.7 = f32[2,64,64]{2,1,0:T(8,128)} copy(f32[2,64,64]{2,1,0:T(8,128)S(1)} %shard_map.55) | data formatting | bytes 65536
